TPU v7x, 512 devices: a whole 4x4x16 slice. The times are simulated.
512 devices in a mesh: seq: 64 (over z, y), head: 8 (over x, core).
Axes of the slice: x: 4, y: 4, z: 16, core: 2. Of those that a mesh axis runs over, the one named last changes fastest.
Arguments:
- queries: bfloat16 [8192, 4096], P('seq', 'head'), may hold values from -6 to 6
- key_rows: bfloat16 [8192, 4096], P('seq', 'head'), may hold values from -6 to 6
- values: bfloat16 [8192, 4096], P('seq', 'head'), may hold values from -32 to 32
- cotangent: bfloat16 [8192, 4096], P(('seq', 'head')), may hold values from -6 to 6
- norm_gain: float32 [4096], replicated, may hold values from 0.5 to 2
Outputs:
- grad_queries: bfloat16 [8192, 4096], P('seq', 'head')
- grad_keys: bfloat16 [8192, 4096], P('seq', 'head')
- grad_values: bfloat16 [8192, 4096], P('seq', 'head')
All inputs are finite; a program needn't handle non-finite values.
Results may differ from a plain program's by a relative error of at most 0.006.
Values may be sent and summed in bfloat16 or wider, within the bound.
A program may use at most 128 MiB of HBM per device.

v0:
```python
import jax
import jax.numpy as jnp
from jax import lax
from jax.sharding import PartitionSpec as P

DH = 128


EPSILON = 1e-06


def entering(value, axis, join, neutral, backward):
    count, mine = (lax.axis_size(axis), lax.axis_index(axis))
    pieces = lax.all_gather(value, axis)
    if backward:
        pieces = pieces[::-1]
        mine = count - 1 - mine
    subtotal = jnp.full_like(value, 0) + jnp.asarray(neutral, value.dtype)

    def turn(position, subtotal):
        longer = join(subtotal, pieces[position])
        return jnp.where(position < mine, longer, subtotal)

    return lax.fori_loop(0, count - 1, turn, subtotal)


def add_states(earlier, later):
    return earlier + later


def local(queries, key_rows, values, cotangent, norm_gain):
    tok_rows = queries.shape[0]
    width_dev = queries.shape[1]
    heads_dev = width_dev // DH
    scaling = DH ** (-0.5)
    query_block = queries.reshape(tok_rows, heads_dev, DH)
    key_block = key_rows.reshape(tok_rows, heads_dev, DH)
    value_block = values.reshape(tok_rows, heads_dev, DH)
    causal = (jnp.arange(tok_rows)[:, None] >= jnp.arange(tok_rows)[None, :])[None]
    local_state = jnp.einsum(
        "thd,the->hde", key_block, value_block, preferred_element_type=jnp.float32
    )
    prefix = entering(local_state, "seq", add_states, jnp.zeros_like(local_state), False)
    prefix_round = prefix.astype(jnp.bfloat16)
    scores = (
        jnp.einsum("thd,shd->hts", query_block, key_block, preferred_element_type=jnp.float32)
        * scaling
    )
    scores_round = jnp.where(causal, scores, jnp.float32(0.0)).astype(jnp.bfloat16)
    inner = jnp.einsum(
        "hts,she->the", scores_round, value_block, preferred_element_type=jnp.float32
    )
    outer = (
        jnp.einsum("thd,hde->the", query_block, prefix_round, preferred_element_type=jnp.float32)
        * scaling
    )
    attended = (inner + outer).astype(jnp.bfloat16).reshape(tok_rows, width_dev)
    token_rows = lax.all_to_all(attended, "head", split_axis=0, concat_axis=1, tiled=True)
    wide = token_rows.astype(jnp.float32)
    scaled_cot = cotangent.astype(jnp.float32) * norm_gain[None, :]
    inverse = lax.rsqrt(jnp.mean(wide * wide, axis=1, keepdims=True) + EPSILON)
    cross = jnp.mean(scaled_cot * wide, axis=1, keepdims=True)
    grad_rows = (inverse * scaled_cot - inverse * inverse * inverse * cross * wide).astype(
        jnp.bfloat16
    )
    grad_attended = lax.all_to_all(grad_rows, "head", split_axis=1, concat_axis=0, tiled=True)
    grad_block = grad_attended.reshape(tok_rows, heads_dev, DH)
    local_grad_state = jnp.einsum(
        "thd,the->hde", query_block, grad_block, preferred_element_type=jnp.float32
    )
    suffix = entering(local_grad_state, "seq", add_states, jnp.zeros_like(local_grad_state), True)
    suffix_round = suffix.astype(jnp.bfloat16)
    grad_scores = (
        jnp.einsum("the,she->hts", grad_block, value_block, preferred_element_type=jnp.float32)
        * scaling
    )
    grad_scores_round = jnp.where(causal, grad_scores, jnp.float32(0.0)).astype(jnp.bfloat16)
    grad_query = jnp.einsum(
        "hts,shd->thd", grad_scores_round, key_block, preferred_element_type=jnp.float32
    )
    grad_query = (
        grad_query
        + jnp.einsum("the,hde->thd", grad_block, prefix_round, preferred_element_type=jnp.float32)
        * scaling
    )
    grad_key = jnp.einsum(
        "hts,thd->shd", grad_scores_round, query_block, preferred_element_type=jnp.float32
    )
    grad_key = (
        grad_key
        + jnp.einsum("she,hde->shd", value_block, suffix_round, preferred_element_type=jnp.float32)
        * scaling
    )
    grad_value = jnp.einsum(
        "hts,the->she", scores_round, grad_block, preferred_element_type=jnp.float32
    )
    grad_value = (
        grad_value
        + jnp.einsum("shd,hde->she", key_block, suffix_round, preferred_element_type=jnp.float32)
        * scaling
    )
    return (
        grad_query.astype(jnp.bfloat16).reshape(tok_rows, width_dev),
        grad_key.astype(jnp.bfloat16).reshape(tok_rows, width_dev),
        grad_value.astype(jnp.bfloat16).reshape(tok_rows, width_dev),
    )


def solution(mesh):
    in_specs = (P("seq", "head"), P("seq", "head"), P("seq", "head"), P(("seq", "head"), None), P())
    out_specs = (P("seq", "head"), P("seq", "head"), P("seq", "head"))
    return jax.shard_map(local, mesh=mesh, in_specs=in_specs, out_specs=out_specs, check_vma=False)
```

profile of v0, /device:TPU:1, one launch (start us, length us, event | category | flops | bytes accessed | tf_op | source)
XLA Modules:
  0.0 575.0 jit_solution(8288017977754764937)
XLA Ops:
  7.2 1.1 copy.156
  8.3 1.8 fusion.18
  10.2 1.1 fusion.9
  11.3 1.1 convolution_bitcast_fusion.3
  12.5 196.9 %all-gather.5.cloned.1.call-done = f32[256,128,128]{2,1,0:T(8,128)} async-done(((f32[4,128,128]{2,1,0:T(8,128)}), f32[256,128,128]{2,1,0:T(8,128)}) %all-gather.5.cloned.1.call-update) | async-done | bytes 16777232 | tf_op jit(solution)/shard_map/all_gather | solution.py:14
  209.4 67.0 %while.28 = (s32[]{:T(128)}, f32[4,128,128]{2,1,0:T(8,128)S(1)}, s32[]{:T(128)}, f32[64,4,128,128]{3,2,1,0:T(8,128)}, s32[]{:T(128)}, /*index=5*/s32[]{:T(128)}) while((s32[]{:T(128)}, f32[4,128,128]{2,1,0:T(8,128)S(1)}, s32[]{:T(128)}, f32[64,4,128,128]{3,2,1,0:T(8,128)}, s32[]{:T(128)}, /*index=5*/s32[]{:T(128)}) %tuple.78), condition=%wide.region_1.2_spmd.clone, body=%wide.region_0.1_spmd.clone.sunk | while | flops 196612 | bytes 786525 | solution.py:24
  210.4 1.0 add_select_fusion.4
  211.5 1.0 add_select_fusion.4
  212.6 1.0 add_select_fusion.4
  213.6 1.0 add_select_fusion.4
  214.7 1.0 add_select_fusion.4
  215.8 1.0 add_select_fusion.4
  216.8 1.0 add_select_fusion.4
  217.9 1.0 add_select_fusion.4
  219.0 1.0 add_select_fusion.4
  220.0 1.0 add_select_fusion.4
  221.1 1.0 add_select_fusion.4
  222.2 1.0 add_select_fusion.4
  223.2 1.0 add_select_fusion.4
  224.3 1.0 add_select_fusion.4
  225.3 1.0 add_select_fusion.4
  226.4 1.0 add_select_fusion.4
  228.5 1.0 add_select_fusion.4
  230.7 1.0 add_select_fusion.4
  232.8 1.0 add_select_fusion.4
  234.9 1.0 add_select_fusion.4
  244.5 1.0 add_select_fusion.4
  246.6 1.0 add_select_fusion.4
  248.8 1.0 add_select_fusion.4
  250.9 1.0 add_select_fusion.4
  253.0 1.0 add_select_fusion.4
  255.1 1.0 add_select_fusion.4
  264.7 1.0 add_select_fusion.4
  266.9 1.0 add_select_fusion.4
  269.0 1.0 add_select_fusion.4
  271.1 1.0 add_select_fusion.4
  273.2 1.0 add_select_fusion.4
  275.4 1.0 add_select_fusion.4
  276.9 10.4 %all_to_all.29 = bf16[8,16,512]{2,1,0:T(8,128)(2,1)S(1)} all-to-all(bf16[8,16,512]{2,1,0:T(8,128)(2,1)S(1)} %all_to_all.22), channel_id=1, replica_groups=mesh['seq'=64,'head'=8] {'head'}, dimensions={0} | all-to-all | bytes 262144 | tf_op jit(solution)/shard_map/all_to_all | solution.py:58
  287.3 1.1 multiply_reduce_fusion
  289.6 8.5 %all_to_all.30 = bf16[16,8,512]{2,0,1:T(8,128)(2,1)S(1)} all-to-all(bf16[16,8,512]{2,0,1:T(8,128)(2,1)S(1)} %bitcast.122), channel_id=1, replica_groups=mesh['seq'=64,'head'=8] {'head'}, dimensions={1} | all-to-all | bytes 262144 | tf_op jit(solution)/shard_map/all_to_all | solution.py:66
  299.4 1.1 fusion.11
  302.1 185.3 %all-gather.7.cloned.1.call-done = f32[256,128,128]{2,1,0:T(8,128)} async-done(((f32[4,128,128]{2,1,0:T(8,128)}), f32[256,128,128]{2,1,0:T(8,128)}) %all-gather.7.cloned.1.call-update) | async-done | bytes 16777232 | tf_op jit(solution)/shard_map/all_gather | solution.py:14
  487.4 11.7 %rev.3 = f32[64,4,128,128]{3,2,1,0:T(8,128)} reverse(f32[64,4,128,128]{3,2,1,0:T(8,128)} %bitcast.117), dimensions={0} | reverse | bytes 33554432 | tf_op jit(solution)/shard_map/rev | solution.py:16
  499.0 67.1 %while.29 = (s32[]{:T(128)}, f32[4,128,128]{2,1,0:T(8,128)S(1)}, s32[]{:T(128)}, f32[64,4,128,128]{3,2,1,0:T(8,128)}, s32[]{:T(128)}, /*index=5*/s32[]{:T(128)}) while((s32[]{:T(128)}, f32[4,128,128]{2,1,0:T(8,128)S(1)}, s32[]{:T(128)}, f32[64,4,128,128]{3,2,1,0:T(8,128)}, s32[]{:T(128)}, /*index=5*/s32[]{:T(128)}) %tuple.71), condition=%wide.region_5.6_spmd.clone, body=%wide.region_4.5_spmd.clone.sunk | while | flops 196612 | bytes 786525 | solution.py:24
  500.1 1.0 add_select_fusion.5
  505.4 1.0 add_select_fusion.5
  506.5 1.0 add_select_fusion.5
  512.9 1.0 add_select_fusion.5
  513.9 1.0 add_select_fusion.5
  519.3 1.0 add_select_fusion.5
  520.3 1.0 add_select_fusion.5
  525.7 1.0 add_select_fusion.5
  526.7 1.0 add_select_fusion.5
  533.1 1.0 add_select_fusion.5
  534.2 1.0 add_select_fusion.5
  539.5 1.0 add_select_fusion.5
  540.6 1.0 add_select_fusion.5
  545.9 1.0 add_select_fusion.5
  547.0 1.0 add_select_fusion.5
  553.3 1.0 add_select_fusion.5
  554.4 1.0 add_select_fusion.5
  559.7 1.0 add_select_fusion.5
  560.8 1.0 add_select_fusion.5
  (110 shorter events, 84.6 us)
Async XLA Ops:
  7.2 3.0 copy-start
  7.2 202.2 %all-gather.5.cloned.1.call-start = ((), (), s32[]{:S(2)}) async-start(), calls=%async_computation.2 | async-start | bytes 17039360 | tf_op jit(solution)/shard_map/all_gather | solution.py:14
  10.1 477.3 %all-gather.7.cloned.1.call-start = ((), (), s32[]{:S(2)}) async-start(), calls=%async_computation.3 | async-start | bytes 17039360 | tf_op jit(solution)/shard_map/all_gather | solution.py:14
  487.4 78.7 %copy-start.2 = (bf16[128,512]{1,0:T(8,128)(2,1)S(1)}, bf16[128,512]{1,0:T(8,128)(2,1)}, u32[]{:S(2)}) copy-start(bf16[128,512]{1,0:T(8,128)(2,1)} %param.10) | copy-start | bytes 393220
  487.4 79.8 %copy-start.1 = (bf16[128,512]{1,0:T(8,128)(2,1)S(1)}, bf16[128,512]{1,0:T(8,128)(2,1)}, u32[]{:S(2)}) copy-start(bf16[128,512]{1,0:T(8,128)(2,1)} %param.11) | copy-start | bytes 393220
Sparse Core Ops, SparseCore 0:
  11.0 198.3 all-gather.4
  299.5 187.8 all-gather.6
where the time goes:
time: 579 us; the launch traced here: 575 us
  waiting for transfers between devices  382 us (66%)
  other arithmetic  133 us (23%)
  blocking collectives  18.9 us (3%)
  local copies, waits for them, and re-layouts  16.3 us (3%)
  between operations  14.2 us (2%)
  matrix products  6.83 us (1%)
    all_gather x2, waiting for transfers between devices, entering(): pieces = lax.all_gather(value, axis)  382 us
    select_n x126, other arithmetic, turn(): return jnp.where(position < mine, longer, subtotal)  131 us
    rev x1, local copies, waits for them, and re-layouts, entering(): pieces = pieces[::-1]  11.7 us
  transfers between devices with their start and end apart: 2, of which 2 were waited for; matrix products, arithmetic and copies ran while one was open for 1% of the time, Pallas kernels for 0%

commit v1 on v0

v1 whole, which is shorter than its diff:
```python
import functools

import jax
import jax.numpy as jnp
from jax import lax
from jax.experimental import pallas as pl
from jax.experimental.pallas import tpu as pltpu
from jax.sharding import PartitionSpec as P

DH = 128
EPSILON = 1e-06
GROUP = 16
HALVES = 2
CORES = 2
MESH = pl.DeviceIdType.MESH
F32 = jnp.float32
BF16 = jnp.bfloat16


def dot(left, right, left_dim, right_dim):
    dims = (((left_dim,), (right_dim,)), ((), ()))
    return lax.dot_general(left, right, dims, preferred_element_type=F32)


def remote(src, dst, send_sem, recv_sem, seq, head):
    return pltpu.make_async_remote_copy(
        src_ref=src,
        dst_ref=dst,
        send_sem=send_sem,
        recv_sem=recv_sem,
        device_id=(seq, head),
        device_id_type=MESH,
    )


def wait_bytes(ref, sem):
    pltpu.make_async_copy(ref, ref, sem).wait()


class Scan:
    def __init__(self, place, backward, state, inbox, part, total, total_in, offset, back, out, sems):
        self.seq, self.head, self.group, self.me, self.size, self.groups = place
        self.backward = backward
        self.state, self.inbox, self.part, self.total = state, inbox, part, total
        self.total_in, self.offset, self.back, self.out = total_in, offset, back, out
        self.s1, self.r1, self.s2, self.r2, self.s3, self.r3 = sems
        self.rows = inbox.shape[2]
        self.core = lax.rem(self.head, CORES)
        self.owner_head = self.head - self.core + CORES - 1
        self.owns = self.core == CORES - 1
        self.row = self.size // 4
        self.mine = self.piece(self.me, self.group)

    def slice_of(self, ref, owner):
        return ref.at[pl.ds(pl.multiple_of(owner * self.rows, self.rows), self.rows)]

    def piece(self, member, group):
        shifted = lax.rem((group + 1) // 2, 2)
        return lax.rem(member + shifted * (self.size // 2), self.size)

    def far_first(self, body):
        here, column = self.me // self.row, lax.rem(self.me, self.row)
        rows = self.size // self.row
        for other in (rows - 1 - here, lax.rem(here + 2, rows), here + 1 - 2 * lax.rem(here, 2), here):
            for step in range(1, self.row + (other is not here)):
                body(other * self.row + lax.rem(column + step, self.row))

    def to_owner(self, owner):
        return remote(
            self.slice_of(self.state, self.piece(owner, self.group)),
            self.inbox.at[self.core, self.me],
            self.s1,
            self.r1.at[self.core],
            self.group * self.size + owner,
            self.owner_head,
        )

    def to_group(self, core, distance, group):
        return remote(
            self.total.at[core],
            self.total_in.at[core, distance - 1],
            self.s2.at[core, distance - 1],
            self.r2.at[core, distance - 1],
            group * self.size + self.piece(self.mine, group),
            self.head,
        )

    def to_member(self, core, member):
        return remote(
            self.back.at[core, member],
            self.slice_of(self.out, self.mine),
            self.s3.at[core],
            self.r3,
            self.group * self.size + member,
            self.head - (CORES - 1) + core,
        )

    def groups_later(self, body):
        for distance in range(1, self.groups):
            if self.backward:
                group, there = self.group - distance, self.group >= distance
            else:
                group, there = self.group + distance, self.group + distance < self.groups
            pl.when(there)(functools.partial(body, distance, group))

    def groups_earlier(self, body):
        for distance in range(1, self.groups):
            if self.backward:
                there = self.group + distance < self.groups
            else:
                there = self.group >= distance
            pl.when(there)(functools.partial(body, distance))

    def by_core(self, first, second):
        pl.when(self.core != CORES - 1)(first)
        pl.when(self.owns)(second)

    def send_state(self):
        self.far_first(lambda owner: self.to_owner(owner).start())

        def keep():
            self.inbox[CORES - 1, self.me] = self.slice_of(self.state, self.mine)[...]

        self.by_core(lambda: self.to_owner(self.me).start(), keep)

    def sum_up(self, core):
        received = self.size - (core == CORES - 1)
        wait_bytes(self.inbox.at[core, pl.ds(0, received)], self.r1.at[core])
        running = jnp.zeros(self.offset.shape[1:], F32)
        order = range(self.size)
        for member in reversed(order) if self.backward else order:
            self.part[core, member] = running
            running = running + self.inbox[core, member].astype(F32)
        self.total[core] = running.astype(BF16)
        self.groups_later(lambda distance, group: self.to_group(core, distance, group).start())
        self.offset[core] = jnp.zeros(self.offset.shape[1:], F32)

    def answer(self, core):
        def add(distance):
            self.to_group(core, distance, self.group).wait_recv()
            self.offset[core] += self.total_in[core, distance - 1].astype(F32)

        self.groups_earlier(add)
        self.back[core] = (self.offset[core][None] + self.part[core]).astype(BF16)
        self.far_first(lambda member: self.to_member(core, member).start())
        if core == CORES - 1:
            self.slice_of(self.out, self.mine)[...] = self.back[core, self.me]
        else:
            self.to_member(core, self.me).start()

    def receive(self):
        def wait(count):
            wait_bytes(self.back.at[0, pl.ds(0, count)], self.r3)

        self.by_core(lambda: wait(self.size), lambda: wait(self.size - 1))

    def drain(self):
        def sent(count):
            wait_bytes(self.inbox.at[0, pl.ds(0, count)], self.s1)

        def owner_sent():
            sent(self.size - 1)
            for core in range(CORES):
                self.groups_later(lambda distance, group: self.to_group(core, distance, group).wait_send())
                wait_bytes(self.back.at[core, pl.ds(0, self.size - (core == CORES - 1))], self.s3.at[core])

        self.by_core(lambda: sent(self.size), owner_sent)


def kernel(n_seq, n_head, size, *refs):
    q_hbm, k_hbm, v_hbm, cot_hbm, gain_hbm, gq, gk, gv = refs[:8]
    q, k, v, cot, gain, cot_block, scaled, inner, scores_t, query_t = refs[8:18]
    attended, grad, key_part, value_part, stat, stat_in = refs[18:24]
    local_sems, cot_send, cot_recv, stat_send, stat_recv = refs[24:29]
    scan_refs = [refs[at : at + 14] for at in range(29, 29 + 14 * 2 * HALVES, 14)]

    seq, head = lax.axis_index("seq"), lax.axis_index("head")
    groups = n_seq // size
    group, me = seq // size, lax.rem(seq, size)
    tokens, width = q.shape
    heads = width // DH
    cot_rows = cot.shape[0]
    scaling = DH ** (-0.5)
    place = (seq, head, group, me, size, groups)
    scans = [Scan(place, i >= HALVES, *own[:8], own[8:]) for i, own in enumerate(scan_refs)]
    forward, backward = scans[:HALVES], scans[HALVES:]
    columns = [slice(h * DH, (h + 1) * DH) for h in range(heads)]
    part_heads = heads // HALVES
    halves = [range(i * part_heads, (i + 1) * part_heads) for i in range(HALVES)]

    loads = [
        pltpu.make_async_copy(src, dst, local_sems.at[i])
        for i, (src, dst) in enumerate(
            [(k_hbm, k), (v_hbm, v), (cot_hbm, cot), (q_hbm, q), (gain_hbm, gain)]
        )
    ]
    for load in loads[:2]:
        load.start()

    barrier = pltpu.get_barrier_semaphore()

    def greet(other_seq, other_head):
        pl.semaphore_signal(
            barrier, inc=1, device_id=(other_seq, other_head), device_id_type=MESH
        )

    def greet_owners():
        forward[0].far_first(lambda member: greet(group * size + member, head + 1))

    def greet_owned():
        for step in range(1, groups):
            other = lax.rem(group + step, groups)
            greet(other * size + forward[0].piece(forward[0].mine, other), head)
        forward[0].far_first(lambda member: greet(group * size + member, head - 1))
        forward[0].far_first(lambda member: greet(group * size + member, head))

    forward[0].by_core(greet_owners, greet_owned)
    for step in range(1, n_head):
        greet(seq, lax.rem(head + step, n_head))
    for load in loads[2:]:
        load.start()

    loads[0].wait()
    loads[1].wait()
    for i, half in enumerate(halves):
        for h in half:
            state = dot(k[:, columns[h]], v[:, columns[h]], 0, 0)
            forward[i].state[columns[h - half[0]], :] = state.astype(BF16)
        if i == 0:
            forward[0].by_core(
                lambda: pl.semaphore_wait(barrier, size - 1 + n_head - 1),
                lambda: pl.semaphore_wait(barrier, 2 * (size - 1) + groups - 1 + n_head - 1),
            )
        forward[i].send_state()

    def cot_columns(to):
        return pl.ds(pl.multiple_of(to * width, width), width)

    def cot_rows_of(owner):
        return cot_block.at[pl.ds(pl.multiple_of(owner * cot_rows, cot_rows), cot_rows)]

    def cot_copy(to, owner):
        return remote(
            cot.at[:, cot_columns(to)],
            cot_rows_of(owner),
            cot_send,
            cot_recv,
            seq,
            to,
        )

    def over_heads(body):
        for step in range(1, n_head):
            body(lax.rem(head + step, n_head))

    loads[2].wait()
    over_heads(lambda to: cot_copy(to, head).start())
    cot_rows_of(head)[...] = cot[:, cot_columns(head)]

    loads[3].wait()
    loads[4].wait()
    rows = lax.broadcasted_iota(jnp.int32, (tokens, tokens), 0)
    cols = lax.broadcasted_iota(jnp.int32, (tokens, tokens), 1)

    def own_block(some):
        for h in some:
            qh, kh, vh = (ref[:, columns[h]] for ref in (q, k, v))
            raw = dot(qh, kh, 1, 1) * scaling
            masked = jnp.where(rows >= cols, raw, 0.0).astype(BF16)
            inner[:, columns[h]] = dot(masked, vh, 1, 0)

    def turned(some):
        for h in some:
            qh, kh = q[:, columns[h]], k[:, columns[h]]
            raw = dot(kh, qh, 1, 1) * scaling
            scores_t[h] = jnp.where(cols >= rows, raw, 0.0).astype(BF16)
            query_t[h] = qh.T

    own_block(halves[0])

    def each(step, some):
        def owner():
            for scan in some:
                for core in range(CORES):
                    step(scan, core)

        pl.when(some[0].owns)(owner)

    each(Scan.sum_up, forward)
    own_block(halves[1])
    wait_bytes(cot.at[:, pl.ds(0, (n_head - 1) * width)], cot_recv)
    scaled[...] = cot_block[...].astype(F32) * gain[:, cot_columns(head)]

    each(Scan.answer, forward)

    turned(range(heads))

    squares = jnp.zeros((tokens, DH), F32)
    products = jnp.zeros((tokens, DH), F32)
    for i, half in enumerate(halves):
        forward[i].receive()
        for h in half:
            prefix = forward[i].out[columns[h - half[0]], :]
            outer = dot(q[:, columns[h]], prefix, 1, 0) * scaling
            rounded = (inner[:, columns[h]] + outer).astype(BF16)
            attended[:, columns[h]] = rounded
            wide = rounded.astype(F32)
            squares = squares + wide * wide
            products = products + wide * scaled[:, columns[h]]
    square_row = jnp.sum(squares.T, axis=0, keepdims=True)
    product_row = jnp.sum(products.T, axis=0, keepdims=True)
    stat_rows = lax.broadcasted_iota(jnp.int32, stat.shape, 0)
    stat[...] = jnp.where(stat_rows == 0, square_row, product_row)

    def stat_copy(to, owner):
        return remote(
            stat, stat_in.at[owner], stat_send, stat_recv, seq, to
        )

    over_heads(lambda to: stat_copy(to, head).start())
    stat_in[head] = stat[...]
    wait_bytes(stat_in.at[pl.ds(0, n_head - 1)], stat_recv)
    summed = jnp.sum(stat_in[...], axis=0) * (1.0 / (n_head * width))
    inverse = lax.rsqrt(summed[0:1, :] + EPSILON)
    slope = inverse * inverse * inverse * summed[1:2, :]
    inverse = jnp.broadcast_to(inverse, (DH, tokens)).T
    slope = jnp.broadcast_to(slope, (DH, tokens)).T

    for i, half in enumerate(halves):
        for h in half:
            wide = attended[:, columns[h]].astype(F32)
            rounded = (inverse * scaled[:, columns[h]] - slope * wide).astype(BF16)
            grad[:, columns[h]] = rounded
            state = dot(query_t[h], rounded, 1, 0)
            backward[i].state[columns[h - half[0]], :] = state.astype(BF16)
        backward[i].send_state()

    def own_grads(h):
        at = columns[h]
        prefix = forward[h // part_heads].out[columns[h % part_heads], :]
        gh, qh, kh, vh = (ref[:, at] for ref in (grad, q, k, v))
        raw = dot(gh, vh, 1, 1) * scaling
        masked = jnp.where(rows >= cols, raw, 0.0).astype(BF16)
        raw = dot(vh, gh, 1, 1) * scaling
        masked_t = jnp.where(cols >= rows, raw, 0.0).astype(BF16)
        outer = dot(gh, prefix, 1, 1) * scaling
        gq[:, at] = (dot(masked, kh, 1, 0) + outer).astype(BF16)
        key_part[:, at] = dot(masked_t, qh, 1, 0)
        value_part[:, at] = dot(scores_t[h], gh, 1, 0)

    for h in range(heads - 2):
        own_grads(h)
    each(Scan.sum_up, backward)
    own_grads(heads - 2)
    each(Scan.answer, backward)
    own_grads(heads - 1)
    for i, half in enumerate(halves):
        backward[i].receive()
        for h in half:
            suffix = backward[i].out[columns[h - half[0]], :]
            outer = dot(v[:, columns[h]], suffix, 1, 1) * scaling
            gk[:, columns[h]] = (key_part[:, columns[h]] + outer).astype(BF16)
            outer = dot(k[:, columns[h]], suffix, 1, 0) * scaling
            gv[:, columns[h]] = (value_part[:, columns[h]] + outer).astype(BF16)

    for scan in scans:
        scan.drain()
    wait_bytes(cot.at[:, pl.ds(0, (n_head - 1) * width)], cot_send)
    wait_bytes(stat_in.at[pl.ds(0, n_head - 1)], stat_send)


def write_out(*refs):
    copies = [pltpu.make_async_copy(refs[i], refs[3 + i], refs[6].at[i]) for i in range(3)]
    for copy in copies:
        copy.start()
    for copy in copies:
        copy.wait()


def solution(mesh):
    n_seq, n_head = mesh.shape["seq"], mesh.shape["head"]
    size = GROUP
    groups = n_seq // size

    def local(queries, key_rows, values, cotangent, norm_gain):
        tokens, width = queries.shape
        heads = width // DH
        part = heads * DH // HALVES
        rows = part // size
        block = pltpu.VMEM((tokens, width), BF16)
        wide = pltpu.VMEM((tokens, width), F32)
        square = pltpu.VMEM((heads, DH, DH), BF16)
        scan = [
            pltpu.VMEM((part, DH), BF16),
            pltpu.VMEM((CORES, size, rows, DH), BF16),
            pltpu.VMEM((CORES, size, rows, DH), F32),
            pltpu.VMEM((CORES, rows, DH), BF16),
            pltpu.VMEM((CORES, groups - 1, rows, DH), BF16),
            pltpu.VMEM((CORES, rows, DH), F32),
            pltpu.VMEM((CORES, size, rows, DH), BF16),
            pltpu.VMEM((part, DH), BF16),
        ]
        dma = pltpu.SemaphoreType.DMA
        scan_sems = [dma, dma((CORES,))] + [dma((CORES, groups - 1))] * 2 + [dma((CORES,)), dma]
        out = pltpu.VMEM((tokens, width), BF16)
        grads = pl.pallas_call(
            functools.partial(kernel, n_seq, n_head, size),
            out_shape=(out, out, out),
            in_specs=[pl.BlockSpec(memory_space=pltpu.HBM)] * 5,
            out_specs=[pl.BlockSpec(memory_space=pltpu.VMEM)] * 3,
            scratch_shapes=[
                block,
                block,
                block,
                pltpu.VMEM(cotangent.shape, BF16),
                pltpu.VMEM((1, norm_gain.shape[0]), F32),
                block,
                wide,
                wide,
                square,
                square,
                block,
                block,
                wide,
                wide,
                pltpu.VMEM((8, tokens), F32),
                pltpu.VMEM((n_head, 8, tokens), F32),
                dma((5,)),
                dma,
                dma,
                dma,
                dma,
                *((scan + scan_sems) * (2 * HALVES)),
            ],
            compiler_params=pltpu.CompilerParams(
                collective_id=0, has_side_effects=True, vmem_limit_bytes=60 * 1024 * 1024
            ),
            cost_estimate=pl.CostEstimate(
                flops=26 * heads * DH**3, bytes_accessed=14 * tokens * width, transcendentals=0
            ),
        )(queries, key_rows, values, cotangent, norm_gain.reshape(1, -1))
        result = jax.ShapeDtypeStruct((tokens, width), BF16)
        return pl.pallas_call(
            write_out,
            out_shape=(result,) * 3,
            in_specs=[pl.BlockSpec(memory_space=pltpu.VMEM)] * 3,
            out_specs=[pl.BlockSpec(memory_space=pltpu.HBM)] * 3,
            scratch_shapes=[dma((3,))],
            compiler_params=pltpu.CompilerParams(vmem_limit_bytes=2 * 1024 * 1024),
        )(*grads)

    return jax.shard_map(
        local,
        mesh=mesh,
        in_specs=(P("seq", "head"), P("seq", "head"), P("seq", "head"), P(("seq", "head"), None), P()),
        out_specs=(P("seq", "head"), P("seq", "head"), P("seq", "head")),
        check_vma=False,
    )
```

time: 579 us -> 53.3 us (0.09)
  waiting for transfers between devices: 382 us -> 0 us
  other arithmetic: 133 us -> 0 us
  Pallas kernels: 0 us -> 52.6 us
  blocking collectives: 18.9 us -> 0 us
  local copies, waits for them, and re-layouts: 16.3 us -> 0 us
  between operations: 14.2 us -> 0.64 us
  matrix products: 6.83 us -> 0 us
    all_gather x2 -> x0, waiting for transfers between devices: 382 us -> none  [entering(): pieces = lax.all_gather(value, axis)]
    select_n x126 -> x0, other arithmetic: 131 us -> none  [turn(): return jnp.where(position < mine, longer, subtotal)]
    pallas_call x0 -> x2, Pallas kernels: none -> 52.6 us  [the longest x1 51.8 us: local(): pl.pallas_call(functools.partial(kernel, n_seq, n_head, size), out_shape=...]
    all_to_all x2 -> x0, blocking collectives: 18.9 us -> none  [the longest x1 10.4 us: local(): lax.all_to_all(attended, 'head', split_axis=0, concat_axis=1, tiled=True)]
    rev x1 -> x0, local copies, waits for them, and re-layouts: 11.7 us -> none  [entering(): pieces = pieces[::-1]]
    dot_general x12 -> x0, matrix products: 6.83 us -> none  [the longest x1 1.79 us: local(): jnp.einsum('thd,the->hde', key_block, value_block, preferred_element_type...]
  transfers between devices with their start and end apart: 2 -> 0, of which waited for: 2 -> 0; matrix products, arithmetic and copies ran while one was open for 1% -> 0% of each run, Pallas kernels for 0% -> 0%
where the time goes in v1:
time: 53.3 us; the launch traced here: 53.2 us
  Pallas kernels  52.6 us (99%)
  between operations  0.64 us (1%)
    pallas_call x1, Pallas kernels, local(): pl.pallas_call(functools.partial(kernel, n_seq, n_head, size), out_shape=...  51.8 us

profile of v1, /device:TPU:1, one launch (start us, length us, event | category | flops | bytes accessed | tf_op | source)
XLA Modules:
  0.0 53.2 jit_solution(7598668766129956575)
XLA Ops:
  0.6 51.8 %shard_map.76 = (bf16[128,512]{1,0:T(8,128)(2,1)S(1)}, bf16[128,512]{1,0:T(8,128)(2,1)S(1)}, bf16[128,512]{1,0:T(8,128)(2,1)S(1)}) custom-call(bf16[128,512]{1,0:T(8,128)(2,1)} %refs_0_.1, bf16[128,512]{1,0:T(8,128)(2,1)} %refs_1_.1, bf16[128,512]{1,0:T(8,128)(2,1)} %refs_2_.1, bf16[16,4096]{1,0:T(8,128)(2,1)} %refs_3_.1, f32[1,4096]{1,0:T(1,128)} %bitcast.1), custom_call_target="tpu_custom_call" | custom-call | flops 218103808 | bytes 917504 | tf_op jit(solution)/shard_map/pallas_call | solution.py:406
  52.4 0.8 %shard_map.77 = (bf16[128,512]{1,0:T(8,128)(2,1)}, bf16[128,512]{1,0:T(8,128)(2,1)}, bf16[128,512]{1,0:T(8,128)(2,1)}) custom-call(bf16[128,512]{1,0:T(8,128)(2,1)S(1)} %get-tuple-element.6.refs_0_, bf16[128,512]{1,0:T(8,128)(2,1)S(1)} %get-tuple-element.7.refs_1_, bf16[128,512]{1,0:T(8,128)(2,1)S(1)} %get-tuple-element.8.refs_2_), custom_call_target="tpu_custom_call" | custom-call | tf_op jit(solution)/shard_map/pallas_call | solution.py:443

commit v2 on v1

--- a/solution.py
+++ b/solution.py
@@ -10,7 +10,7 @@
 DH = 128
 EPSILON = 1e-06
 GROUP = 16
-HALVES = 2
+HALVES = 1
 CORES = 2
 MESH = pl.DeviceIdType.MESH
 F32 = jnp.float32
@@ -58,10 +58,11 @@
         shifted = lax.rem((group + 1) // 2, 2)
         return lax.rem(member + shifted * (self.size // 2), self.size)
 
-    def far_first(self, body):
+    def far_first(self, body, planes=slice(None)):
         here, column = self.me // self.row, lax.rem(self.me, self.row)
         rows = self.size // self.row
-        for other in (rows - 1 - here, lax.rem(here + 2, rows), here + 1 - 2 * lax.rem(here, 2), here):
+        others = (rows - 1 - here, lax.rem(here + 2, rows), here + 1 - 2 * lax.rem(here, 2), here)
+        for other in others[planes]:
             for step in range(1, self.row + (other is not here)):
                 body(other * self.row + lax.rem(column + step, self.row))
 
@@ -135,6 +136,13 @@
         self.groups_later(lambda distance, group: self.to_group(core, distance, group).start())
         self.offset[core] = jnp.zeros(self.offset.shape[1:], F32)
 
+    def near(self, core):
+        self.far_first(lambda member: self.to_member(core, member).start(), slice(2, 4))
+        if core == CORES - 1:
+            self.slice_of(self.out, self.mine)[...] = self.back[core, self.me]
+        else:
+            self.to_member(core, self.me).start()
+
     def answer(self, core):
         def add(distance):
             self.to_group(core, distance, self.group).wait_recv()
@@ -142,11 +150,7 @@
 
         self.groups_earlier(add)
         self.back[core] = (self.offset[core][None] + self.part[core]).astype(BF16)
-        self.far_first(lambda member: self.to_member(core, member).start())
-        if core == CORES - 1:
-            self.slice_of(self.out, self.mine)[...] = self.back[core, self.me]
-        else:
-            self.to_member(core, self.me).start()
+        self.far_first(lambda member: self.to_member(core, member).start(), slice(0, 2))
 
     def receive(self):
         def wait(count):
@@ -276,22 +280,23 @@
             scores_t[h] = jnp.where(cols >= rows, raw, 0.0).astype(BF16)
             query_t[h] = qh.T
 
-    own_block(halves[0])
-
-    def each(step, some):
+    own_block(range(heads // 2))
+
+    def each(scan, *steps):
         def owner():
-            for scan in some:
-                for core in range(CORES):
+            order = range(CORES)
+            for step in steps:
+                for core in reversed(order) if scan.backward else order:
                     step(scan, core)
 
-        pl.when(some[0].owns)(owner)
-
-    each(Scan.sum_up, forward)
-    own_block(halves[1])
+        pl.when(scan.owns)(owner)
+
+    each(forward[0], Scan.sum_up)
+    own_block(range(heads // 2, heads))
     wait_bytes(cot.at[:, pl.ds(0, (n_head - 1) * width)], cot_recv)
     scaled[...] = cot_block[...].astype(F32) * gain[:, cot_columns(head)]
 
-    each(Scan.answer, forward)
+    each(forward[0], Scan.answer, Scan.near)
 
     turned(range(heads))
 
@@ -350,9 +355,9 @@
 
     for h in range(heads - 2):
         own_grads(h)
-    each(Scan.sum_up, backward)
+    each(backward[0], Scan.sum_up)
     own_grads(heads - 2)
-    each(Scan.answer, backward)
+    each(backward[0], Scan.answer, Scan.near)
     own_grads(heads - 1)
     for i, half in enumerate(halves):
         backward[i].receive()

time: 53.3 us -> 51.8 us (0.972)
  Pallas kernels: 52.6 us -> 51 us
    pallas_call x1, Pallas kernels: 51.8 us -> 50.2 us  [local(): pl.pallas_call(functools.partial(kernel, n_seq, n_head, size), out_shape=...]
where the time goes in v2:
time: 51.8 us; the launch traced here: 51.6 us
  Pallas kernels  51 us (98%)
  between operations  0.64 us (1%)
    pallas_call x1, Pallas kernels, local(): pl.pallas_call(functools.partial(kernel, n_seq, n_head, size), out_shape=...  50.2 us

profile of v2, /device:TPU:1, one launch (start us, length us, event | category | flops | bytes accessed | tf_op | source)
XLA Modules:
  0.0 51.6 jit_solution(11047560341489312950)
XLA Ops:
  0.6 50.2 %shard_map.76 = (bf16[128,512]{1,0:T(8,128)(2,1)S(1)}, bf16[128,512]{1,0:T(8,128)(2,1)S(1)}, bf16[128,512]{1,0:T(8,128)(2,1)S(1)}) custom-call(bf16[128,512]{1,0:T(8,128)(2,1)} %refs_0_.1, bf16[128,512]{1,0:T(8,128)(2,1)} %refs_1_.1, bf16[128,512]{1,0:T(8,128)(2,1)} %refs_2_.1, bf16[16,4096]{1,0:T(8,128)(2,1)} %refs_3_.1, f32[1,4096]{1,0:T(1,128)} %bitcast.1), custom_call_target="tpu_custom_call" | custom-call | flops 218103808 | bytes 917504 | tf_op jit(solution)/shard_map/pallas_call | solution.py:411
  50.8 0.8 %shard_map.77 = (bf16[128,512]{1,0:T(8,128)(2,1)}, bf16[128,512]{1,0:T(8,128)(2,1)}, bf16[128,512]{1,0:T(8,128)(2,1)}) custom-call(bf16[128,512]{1,0:T(8,128)(2,1)S(1)} %get-tuple-element.6.refs_0_, bf16[128,512]{1,0:T(8,128)(2,1)S(1)} %get-tuple-element.7.refs_1_, bf16[128,512]{1,0:T(8,128)(2,1)S(1)} %get-tuple-element.8.refs_2_), custom_call_target="tpu_custom_call" | custom-call | tf_op jit(solution)/shard_map/pallas_call | solution.py:448

commit v3 on v2

--- a/solution.py
+++ b/solution.py
@@ -127,17 +127,30 @@
     def sum_up(self, core):
         received = self.size - (core == CORES - 1)
         wait_bytes(self.inbox.at[core, pl.ds(0, received)], self.r1.at[core])
+        total = jnp.zeros(self.offset.shape[1:], F32)
+        for member in range(self.size):
+            total = total + self.inbox[core, member].astype(F32)
+        self.total[core] = total.astype(BF16)
+        self.groups_later(lambda distance, group: self.to_group(core, distance, group).start())
+        self.offset[core] = jnp.zeros(self.offset.shape[1:], F32)
+
+    def add_up(self, core):
         running = jnp.zeros(self.offset.shape[1:], F32)
         order = range(self.size)
         for member in reversed(order) if self.backward else order:
             self.part[core, member] = running
             running = running + self.inbox[core, member].astype(F32)
-        self.total[core] = running.astype(BF16)
-        self.groups_later(lambda distance, group: self.to_group(core, distance, group).start())
-        self.offset[core] = jnp.zeros(self.offset.shape[1:], F32)
+
+    def in_order(self, body):
+        here, column = self.me // self.row, lax.rem(self.me, self.row)
+        for other in range(self.size // self.row):
+            pl.when(here != other)(functools.partial(body, other * self.row + column))
+            for step in range(1, self.row):
+                body(other * self.row + lax.rem(column + step, self.row))
 
     def near(self, core):
-        self.far_first(lambda member: self.to_member(core, member).start(), slice(2, 4))
+        if not self.backward:
+            self.far_first(lambda member: self.to_member(core, member).start(), slice(2, 4))
         if core == CORES - 1:
             self.slice_of(self.out, self.mine)[...] = self.back[core, self.me]
         else:
@@ -150,7 +163,10 @@
 
         self.groups_earlier(add)
         self.back[core] = (self.offset[core][None] + self.part[core]).astype(BF16)
-        self.far_first(lambda member: self.to_member(core, member).start(), slice(0, 2))
+        if self.backward:
+            self.in_order(lambda member: self.to_member(core, member).start())
+        else:
+            self.far_first(lambda member: self.to_member(core, member).start(), slice(0, 2))
 
     def receive(self):
         def wait(count):
@@ -291,7 +307,7 @@
 
         pl.when(scan.owns)(owner)
 
-    each(forward[0], Scan.sum_up)
+    each(forward[0], Scan.sum_up, Scan.add_up)
     own_block(range(heads // 2, heads))
     wait_bytes(cot.at[:, pl.ds(0, (n_head - 1) * width)], cot_recv)
     scaled[...] = cot_block[...].astype(F32) * gain[:, cot_columns(head)]
@@ -355,7 +371,7 @@
 
     for h in range(heads - 2):
         own_grads(h)
-    each(backward[0], Scan.sum_up)
+    each(backward[0], Scan.sum_up, Scan.add_up)
     own_grads(heads - 2)
     each(backward[0], Scan.answer, Scan.near)
     own_grads(heads - 1)

time: 51.8 us -> 51.1 us (0.986)
  Pallas kernels: 51 us -> 50.3 us
    pallas_call x1, Pallas kernels: 50.2 us -> 49.5 us  [local(): pl.pallas_call(functools.partial(kernel, n_seq, n_head, size), out_shape=...]
where the time goes in v3:
time: 51.1 us; the launch traced here: 50.9 us
  Pallas kernels  50.3 us (98%)
  between operations  0.64 us (1%)
    pallas_call x1, Pallas kernels, local(): pl.pallas_call(functools.partial(kernel, n_seq, n_head, size), out_shape=...  49.5 us

profile of v3, /device:TPU:1, one launch (start us, length us, event | category | flops | bytes accessed | tf_op | source)
XLA Modules:
  0.0 50.9 jit_solution(16449388276330281955)
XLA Ops:
  0.6 49.5 %shard_map.76 = (bf16[128,512]{1,0:T(8,128)(2,1)S(1)}, bf16[128,512]{1,0:T(8,128)(2,1)S(1)}, bf16[128,512]{1,0:T(8,128)(2,1)S(1)}) custom-call(bf16[128,512]{1,0:T(8,128)(2,1)} %refs_0_.1, bf16[128,512]{1,0:T(8,128)(2,1)} %refs_1_.1, bf16[128,512]{1,0:T(8,128)(2,1)} %refs_2_.1, bf16[16,4096]{1,0:T(8,128)(2,1)} %refs_3_.1, f32[1,4096]{1,0:T(1,128)} %bitcast.1), custom_call_target="tpu_custom_call" | custom-call | flops 218103808 | bytes 917504 | tf_op jit(solution)/shard_map/pallas_call | solution.py:427
  50.2 0.8 %shard_map.77 = (bf16[128,512]{1,0:T(8,128)(2,1)}, bf16[128,512]{1,0:T(8,128)(2,1)}, bf16[128,512]{1,0:T(8,128)(2,1)}) custom-call(bf16[128,512]{1,0:T(8,128)(2,1)S(1)} %get-tuple-element.6.refs_0_, bf16[128,512]{1,0:T(8,128)(2,1)S(1)} %get-tuple-element.7.refs_1_, bf16[128,512]{1,0:T(8,128)(2,1)S(1)} %get-tuple-element.8.refs_2_), custom_call_target="tpu_custom_call" | custom-call | tf_op jit(solution)/shard_map/pallas_call | solution.py:464

commit v4 on v3

--- a/solution.py
+++ b/solution.py
@@ -58,13 +58,14 @@
         shifted = lax.rem((group + 1) // 2, 2)
         return lax.rem(member + shifted * (self.size // 2), self.size)
 
-    def far_first(self, body, planes=slice(None)):
+    def far_first(self, *bodies, planes=slice(None)):
         here, column = self.me // self.row, lax.rem(self.me, self.row)
         rows = self.size // self.row
         others = (rows - 1 - here, lax.rem(here + 2, rows), here + 1 - 2 * lax.rem(here, 2), here)
         for other in others[planes]:
             for step in range(1, self.row + (other is not here)):
-                body(other * self.row + lax.rem(column + step, self.row))
+                for body in bodies:
+                    body(other * self.row + lax.rem(column + step, self.row))
 
     def to_owner(self, owner):
         return remote(
@@ -150,7 +151,7 @@
 
     def near(self, core):
         if not self.backward:
-            self.far_first(lambda member: self.to_member(core, member).start(), slice(2, 4))
+            self.far_first(lambda member: self.to_member(core, member).start(), planes=slice(2, 4))
         if core == CORES - 1:
             self.slice_of(self.out, self.mine)[...] = self.back[core, self.me]
         else:
@@ -166,7 +167,7 @@
         if self.backward:
             self.in_order(lambda member: self.to_member(core, member).start())
         else:
-            self.far_first(lambda member: self.to_member(core, member).start(), slice(0, 2))
+            self.far_first(lambda member: self.to_member(core, member).start(), planes=slice(0, 2))
 
     def receive(self):
         def wait(count):
@@ -231,8 +232,10 @@
         for step in range(1, groups):
             other = lax.rem(group + step, groups)
             greet(other * size + forward[0].piece(forward[0].mine, other), head)
-        forward[0].far_first(lambda member: greet(group * size + member, head - 1))
-        forward[0].far_first(lambda member: greet(group * size + member, head))
+        forward[0].far_first(
+            lambda member: greet(group * size + member, head),
+            lambda member: greet(group * size + member, head - 1),
+        )
 
     forward[0].by_core(greet_owners, greet_owned)
     for step in range(1, n_head):

time: 51.1 us -> 51 us (level)
  no operation moved by 1% of the time
where the time goes in v4:
time: 51 us; the launch traced here: 50.9 us
  Pallas kernels  50.2 us (98%)
  between operations  0.64 us (1%)
    pallas_call x1, Pallas kernels, local(): pl.pallas_call(functools.partial(kernel, n_seq, n_head, size), out_shape=...  49.5 us

profile of v4, /device:TPU:1, one launch (start us, length us, event | category | flops | bytes accessed | tf_op | source)
XLA Modules:
  0.0 50.9 jit_solution(9139078020334920390)
XLA Ops:
  0.6 49.5 %shard_map.76 = (bf16[128,512]{1,0:T(8,128)(2,1)S(1)}, bf16[128,512]{1,0:T(8,128)(2,1)S(1)}, bf16[128,512]{1,0:T(8,128)(2,1)S(1)}) custom-call(bf16[128,512]{1,0:T(8,128)(2,1)} %refs_0_.1, bf16[128,512]{1,0:T(8,128)(2,1)} %refs_1_.1, bf16[128,512]{1,0:T(8,128)(2,1)} %refs_2_.1, bf16[16,4096]{1,0:T(8,128)(2,1)} %refs_3_.1, f32[1,4096]{1,0:T(1,128)} %bitcast.1), custom_call_target="tpu_custom_call" | custom-call | flops 218103808 | bytes 917504 | tf_op jit(solution)/shard_map/pallas_call | solution.py:430
  50.1 0.8 %shard_map.77 = (bf16[128,512]{1,0:T(8,128)(2,1)}, bf16[128,512]{1,0:T(8,128)(2,1)}, bf16[128,512]{1,0:T(8,128)(2,1)}) custom-call(bf16[128,512]{1,0:T(8,128)(2,1)S(1)} %get-tuple-element.6.refs_0_, bf16[128,512]{1,0:T(8,128)(2,1)S(1)} %get-tuple-element.7.refs_1_, bf16[128,512]{1,0:T(8,128)(2,1)S(1)} %get-tuple-element.8.refs_2_), custom_call_target="tpu_custom_call" | custom-call | tf_op jit(solution)/shard_map/pallas_call | solution.py:467

commit v5 on v4

--- a/solution.py
+++ b/solution.py
@@ -118,12 +118,20 @@
         pl.when(self.owns)(second)
 
     def send_state(self):
-        self.far_first(lambda owner: self.to_owner(owner).start())
-
-        def keep():
+        far, near = slice(None), slice(None, None, -1)
+
+        def send(planes):
+            self.far_first(lambda owner: self.to_owner(owner).start(), planes=planes)
+
+        def first():
+            send(near if self.backward else far)
+            self.to_owner(self.me).start()
+
+        def second():
+            send(far if self.backward else near)
             self.inbox[CORES - 1, self.me] = self.slice_of(self.state, self.mine)[...]
 
-        self.by_core(lambda: self.to_owner(self.me).start(), keep)
+        self.by_core(first, second)
 
     def sum_up(self, core):
         received = self.size - (core == CORES - 1)

time: 51 us -> 50.3 us (0.986)
  Pallas kernels: 50.2 us -> 49.5 us
    pallas_call x1, Pallas kernels: 49.5 us -> 48.8 us  [local(): pl.pallas_call(functools.partial(kernel, n_seq, n_head, size), out_shape=...]
where the time goes in v5:
time: 50.3 us; the launch traced here: 50.2 us
  Pallas kernels  49.5 us (98%)
  between operations  0.64 us (1%)
    pallas_call x1, Pallas kernels, local(): pl.pallas_call(functools.partial(kernel, n_seq, n_head, size), out_shape=...  48.8 us

profile of v5, /device:TPU:1, one launch (start us, length us, event | category | flops | bytes accessed | tf_op | source)
XLA Modules:
  0.0 50.2 jit_solution(3740929640717892363)
XLA Ops:
  0.6 48.8 %shard_map.76 = (bf16[128,512]{1,0:T(8,128)(2,1)S(1)}, bf16[128,512]{1,0:T(8,128)(2,1)S(1)}, bf16[128,512]{1,0:T(8,128)(2,1)S(1)}) custom-call(bf16[128,512]{1,0:T(8,128)(2,1)} %refs_0_.1, bf16[128,512]{1,0:T(8,128)(2,1)} %refs_1_.1, bf16[128,512]{1,0:T(8,128)(2,1)} %refs_2_.1, bf16[16,4096]{1,0:T(8,128)(2,1)} %refs_3_.1, f32[1,4096]{1,0:T(1,128)} %bitcast.1), custom_call_target="tpu_custom_call" | custom-call | flops 218103808 | bytes 917504 | tf_op jit(solution)/shard_map/pallas_call | solution.py:438
  49.4 0.8 %shard_map.77 = (bf16[128,512]{1,0:T(8,128)(2,1)}, bf16[128,512]{1,0:T(8,128)(2,1)}, bf16[128,512]{1,0:T(8,128)(2,1)}) custom-call(bf16[128,512]{1,0:T(8,128)(2,1)S(1)} %get-tuple-element.6.refs_0_, bf16[128,512]{1,0:T(8,128)(2,1)S(1)} %get-tuple-element.7.refs_1_, bf16[128,512]{1,0:T(8,128)(2,1)S(1)} %get-tuple-element.8.refs_2_), custom_call_target="tpu_custom_call" | custom-call | tf_op jit(solution)/shard_map/pallas_call | solution.py:475

commit v6 on v5

--- a/solution.py
+++ b/solution.py
@@ -159,7 +159,7 @@
 
     def near(self, core):
         if not self.backward:
-            self.far_first(lambda member: self.to_member(core, member).start(), planes=slice(2, 4))
+            self.far_first(lambda member: self.to_member(core, member).start(), planes=slice(2 - 2 * core, 4 - 2 * core))
         if core == CORES - 1:
             self.slice_of(self.out, self.mine)[...] = self.back[core, self.me]
         else:
@@ -175,7 +175,7 @@
         if self.backward:
             self.in_order(lambda member: self.to_member(core, member).start())
         else:
-            self.far_first(lambda member: self.to_member(core, member).start(), planes=slice(0, 2))
+            self.far_first(lambda member: self.to_member(core, member).start(), planes=slice(2 * core, 2 + 2 * core))
 
     def receive(self):
         def wait(count):

time: 50.3 us -> 50.5 us (level)
  no operation moved by 1% of the time
where the time goes in v6:
time: 50.5 us; the launch traced here: 50.4 us
  Pallas kernels  49.8 us (99%)
  between operations  0.64 us (1%)
    pallas_call x1, Pallas kernels, local(): pl.pallas_call(functools.partial(kernel, n_seq, n_head, size), out_shape=...  49 us

profile of v6, /device:TPU:1, one launch (start us, length us, event | category | flops | bytes accessed | tf_op | source)
XLA Modules:
  0.0 50.4 jit_solution(18026192028829276663)
XLA Ops:
  0.6 49.0 %shard_map.76 = (bf16[128,512]{1,0:T(8,128)(2,1)S(1)}, bf16[128,512]{1,0:T(8,128)(2,1)S(1)}, bf16[128,512]{1,0:T(8,128)(2,1)S(1)}) custom-call(bf16[128,512]{1,0:T(8,128)(2,1)} %refs_0_.1, bf16[128,512]{1,0:T(8,128)(2,1)} %refs_1_.1, bf16[128,512]{1,0:T(8,128)(2,1)} %refs_2_.1, bf16[16,4096]{1,0:T(8,128)(2,1)} %refs_3_.1, f32[1,4096]{1,0:T(1,128)} %bitcast.1), custom_call_target="tpu_custom_call" | custom-call | flops 218103808 | bytes 917504 | tf_op jit(solution)/shard_map/pallas_call | solution.py:438
  49.6 0.8 %shard_map.77 = (bf16[128,512]{1,0:T(8,128)(2,1)}, bf16[128,512]{1,0:T(8,128)(2,1)}, bf16[128,512]{1,0:T(8,128)(2,1)}) custom-call(bf16[128,512]{1,0:T(8,128)(2,1)S(1)} %get-tuple-element.6.refs_0_, bf16[128,512]{1,0:T(8,128)(2,1)S(1)} %get-tuple-element.7.refs_1_, bf16[128,512]{1,0:T(8,128)(2,1)S(1)} %get-tuple-element.8.refs_2_), custom_call_target="tpu_custom_call" | custom-call | tf_op jit(solution)/shard_map/pallas_call | solution.py:475
